TPU v7x, 32 devices: a whole 2x2x4 slice. The times are simulated.
32 devices in a mesh: tile: 8 (over z, y), code: 4 (over x, core).
Axes of the slice: x: 2, y: 2, z: 4, core: 2. Of those that a mesh axis runs over, the one named last changes fastest.
Arguments:
- features: bfloat16 [8, 4, 1, 16, 32, 512], P('tile', 'code'), may hold values from -6 to 6
- w_first: bfloat16 [3, 3, 512, 512], replicated, may hold values from -0.09375 to 0.09375
- b_first: float32 [512], replicated, may hold values from -3 to 3
- w_latent: bfloat16 [3, 3, 512, 256], replicated, may hold values from -0.09375 to 0.09375
- b_latent: float32 [256], replicated, may hold values from -3 to 3
- codebook: bfloat16 [65536, 256], P(('tile', 'code')), may hold values from -6 to 6
- upstream: bfloat16 [8, 4, 1, 16, 32, 256], P('tile', 'code'), may hold values from -6 to 6
- owner: int32 [8, 4, 512, 1], P('tile', 'code'), may hold values from 0 to 31; in each aligned block of 512 rows (0 to 511, 512 to 1023, ..., all dimensions but the last counted through in order) at most 32 rows name the same one
- local_code: int32 [8, 4, 512], P('tile', 'code'), may hold values from 0 to 2047
Outputs:
- grad_latent: bfloat16 [8, 4, 1, 16, 32, 256], P('tile', 'code')
- row_loss: float32 [1, 128], P(None, 'tile')
- code_sums: float32 [65536, 256], P(('tile', 'code'))
- code_counts: float32 [65536], P(('tile', 'code'))
Inputs may be any that keep to these rules, and one draw needn't show every extreme that they name: Among the tokens of one tile, at most 32 name the same owner, and exactly 32 do for some owner.
All inputs are finite; a program needn't handle non-finite values.
Results may differ from a plain program's by a relative error of at most 0.0025.
Values may be sent and summed in bfloat16 or wider, within the bound.
A program may use at most 64 MiB of HBM per device.

v0:
```python
import jax
import jax.numpy as jnp
from jax import lax
from jax.sharding import PartitionSpec as P

BETA = 0.25


def extended(array, sides, width):
    for axis, dim in sides:
        devices, length = (lax.axis_size(axis), array.shape[dim])
        up = [(i, (i + 1) % devices) for i in range(devices - 1)]
        down = [(j, i) for i, j in up]
        last = lax.slice_in_dim(array, length - width, length, axis=dim)
        first = lax.slice_in_dim(array, 0, width, axis=dim)
        before = lax.ppermute(last, axis, up)
        after = lax.ppermute(first, axis, down)
        array = jnp.concatenate([before, array, after], axis=dim)
    return array


def convolve(padded, weight):
    return lax.conv_general_dilated(
        padded,
        weight,
        (1, 1),
        "VALID",
        dimension_numbers=("NHWC", "HWIO", "NHWC"),
        preferred_element_type=jnp.float32,
    )


def send_joint(requests, parcel):
    return (
        lax.all_to_all(requests, ("tile", "code"), split_axis=0, concat_axis=0, tiled=True),
        lax.all_to_all(
            parcel.astype(jnp.bfloat16), ("tile", "code"), split_axis=0, concat_axis=0, tiled=True
        ).astype(parcel.dtype),
    )


def send_back(answer):
    return lax.all_to_all(answer, ("tile", "code"), split_axis=0, concat_axis=0, tiled=True)


def compute_latent(frames, w_first, b_first, w_latent, b_latent):
    padded = extended(frames, (("tile", 1), ("code", 2)), 1)
    hidden = jax.nn.silu(convolve(padded, w_first) + b_first).astype(jnp.bfloat16)
    padded_hidden = extended(hidden, (("tile", 1), ("code", 2)), 1)
    return convolve(padded_hidden, w_latent) + b_latent


def lookup(asked, codebook, latent_width, device_count, capacity):
    flat_asked = asked.reshape(-1)
    safe_index = jnp.maximum(flat_asked, 0)
    answer = codebook[safe_index].reshape(device_count, capacity, latent_width)
    return send_back(answer)


def shards(features, w_first, b_first, w_latent, b_latent, codebook, upstream, owner, local_code):
    tile_count = lax.axis_size("tile")
    code_count = lax.axis_size("code")
    device_count = tile_count * code_count
    frames = features[0, 0]
    frame_count, row_count, col_count, _ = frames.shape
    latent_width = w_latent.shape[3]
    token_count = owner.shape[2]
    capacity = max(2, 2 * token_count // device_count)
    target = owner[0, 0, :, 0]
    within = local_code[0, 0]
    member = (target[:, None] == jnp.arange(device_count, dtype=jnp.int32)[None, :]).astype(
        jnp.int32
    )
    earlier = jnp.cumsum(member, axis=0) - member
    place = target * capacity + jnp.sum(earlier * member, axis=1)
    requests = (
        jnp.full((device_count * capacity,), -1, jnp.int32)
        .at[place]
        .set(within)
        .reshape(device_count, capacity)
    )
    latent = compute_latent(frames, w_first, b_first, w_latent, b_latent)
    flat = latent.reshape(token_count, latent_width)
    parcel = jnp.zeros((device_count * capacity, latent_width), jnp.float32).at[place].set(flat)
    flat_latent, parcel = (flat, parcel.reshape(device_count, capacity, latent_width))
    asked, arrived = send_joint(requests, parcel)
    returned = lookup(asked, codebook, latent_width, device_count, capacity)
    flat_asked = asked.reshape(-1)
    safe_index = jnp.maximum(flat_asked, 0)
    weights = (flat_asked >= 0).astype(jnp.float32)
    code_sums = (
        jnp.zeros((codebook.shape[0], latent_width), jnp.float32)
        .at[safe_index]
        .add(arrived.reshape(-1, latent_width) * weights[:, None])
    )
    code_counts = jnp.zeros((codebook.shape[0],), jnp.float32).at[safe_index].add(weights)
    chosen = returned.reshape(device_count * capacity, latent_width)[place].astype(jnp.float32)
    differ = flat_latent - chosen
    grad_flat = (
        upstream.reshape(token_count, latent_width).astype(jnp.float32) + 2.0 * BETA * differ
    )
    grad_latent = grad_flat.astype(jnp.bfloat16).reshape(upstream.shape)
    squared = jnp.sum(
        (differ * differ).reshape(frame_count, row_count, col_count, latent_width), axis=(2, 3)
    )
    total = lax.psum(squared, "code")
    row_loss = BETA * total / (col_count * code_count * latent_width)
    return (grad_latent, row_loss, code_sums, code_counts)


def solution(mesh):
    in_specs = (
        P("tile", "code", None, None, None, None),
        P(),
        P(),
        P(),
        P(),
        P(("tile", "code"), None),
        P("tile", "code", None, None, None, None),
        P("tile", "code", None, None),
        P("tile", "code", None),
    )
    out_specs = (
        P("tile", "code", None, None, None, None),
        P(None, "tile"),
        P(("tile", "code"), None),
        P(("tile", "code")),
    )
    return jax.shard_map(shards, mesh=mesh, in_specs=in_specs, out_specs=out_specs, check_vma=False)
```

profile of v0, /device:TPU:0, one launch (start us, length us, event | category | flops | bytes accessed | tf_op | source)
XLA Modules:
  0.0 123.2 jit_solution(14409847273048516652)
XLA Ops:
  0.7 0.8 fusion.31
  1.5 1.2 reduce-window.6
  2.9 0.8 fusion.30
  3.7 0.7 compare_select_fusion
  4.4 2.6 %scatter_custom_fusion = s32[1024]{0:T(1024)S(1)} fusion(s32[512]{0:T(512)S(1)} %bitcast.87, s32[512]{0:T(512)} %bitcast.92, s32[]{:T(128)} %constant.9.clone.1), kind=kCustom, calls=%fused_computation.66 | custom fusion | bytes 4608 | tf_op jit(solution)/shard_map/scatter | solution.py:79
  7.0 0.7 all_to_all.12
  7.7 7.3 %all-to-all-start = ((s32[32,1,32]{2,1,0:T(1,128)}), s32[32,1,32]{2,1,0:T(1,128)S(1)}, u32[]{:S(2)}, u32[]{:S(2)}) async-start(s32[32,1,32]{2,1,0:T(1,128)} %all_to_all.12), calls=%async_computation | async-start | bytes 32768 | tf_op jit(solution)/shard_map/all_to_all | solution.py:35
  15.0 1.4 %fusion.44 = (bf16[1,1,32,512]{3,2,1,0:T(8,128)(2,1)S(1)}, bf16[1,1,32,512]{3,2,1,0:T(8,128)(2,1)}) fusion(bf16[1,16,32,512]{3,2,1,0:T(8,128)(2,1)} %bitcast.78), kind=kLoop, calls=%fused_computation.76 | loop fusion | bytes 131072 | tf_op jit(solution)/shard_map/slice | solution.py:14
  16.4 1.3 %collective-permute-start.1 = (bf16[1,1,32,512]{3,2,1,0:T(8,128)(2,1)}, bf16[1,1,32,512]{3,2,1,0:T(8,128)(2,1)S(1)}, u32[]{:S(2)}, u32[]{:S(2)}) collective-permute-start(bf16[1,1,32,512]{3,2,1,0:T(8,128)(2,1)} %get-tuple-element.19), channel_id=1, source_target_pairs={{4,0},{8,4},{12,8},{16,12},{20,16},{24,20},{28,24},{5,1},{9,5},{13... | collective-permute-start | bytes 98312 | tf_op jit(solution)/shard_map/ppermute | solution.py:17
  17.7 4.5 %collective-permute-start = (bf16[1,1,32,512]{3,2,1,0:T(8,128)(2,1)S(1)}, bf16[1,1,32,512]{3,2,1,0:T(8,128)(2,1)S(1)}, u32[]{:S(2)}, u32[]{:S(2)}) collective-permute-start(bf16[1,1,32,512]{3,2,1,0:T(8,128)(2,1)S(1)} %get-tuple-element.18), channel_id=1, source_target_pairs={{0,4},{4,8},{8,12},{12,16},{16,20},{20,24},{24,28},{1,5},{5,9},{9,... | collective-permute-start | bytes 98312 | tf_op jit(solution)/shard_map/ppermute | solution.py:16
  22.4 1.4 %collective-permute-done = bf16[1,1,32,512]{3,2,1,0:T(8,128)(2,1)S(1)} collective-permute-done((bf16[1,1,32,512]{3,2,1,0:T(8,128)(2,1)S(1)}, bf16[1,1,32,512]{3,2,1,0:T(8,128)(2,1)S(1)}, u32[]{:S(2)}, u32[]{:S(2)}) %collective-permute-start) | collective-permute-done | bytes 32800 | tf_op jit(solution)/shard_map/ppermute | solution.py:16
  23.8 1.7 %pad_maximum_fusion.2 = (bf16[1,18,1,512]{3,2,1,0:T(2,128)(2,1)}, bf16[1,18,1,512]{3,2,1,0:T(2,128)(2,1)}) fusion(bf16[1,1,32,512]{3,2,1,0:T(8,128)(2,1)S(1)} %collective-permute-done.1, bf16[1,16,32,512]{3,2,1,0:T(8,128)(2,1)} %bitcast.79, bf16[1,1,32,512]{3,2,1,0:T(8,128)(2,1)S(1)} %collective-permute-done), kind=kLoop, calls=%fused_computation.54 | loop fusion | flops 110592 | bytes 626688 | tf_op jit(solution)/shard_map/slice | solution.py:14
  25.5 1.3 %collective-permute-start.3 = (bf16[1,18,1,512]{3,2,1,0:T(2,128)(2,1)}, bf16[1,18,1,512]{3,2,1,0:T(2,128)(2,1)S(1)}, u32[]{:S(2)}, u32[]{:S(2)}) collective-permute-start(bf16[1,18,1,512]{3,2,1,0:T(2,128)(2,1)} %get-tuple-element.17), channel_id=1, source_target_pairs={{1,0},{2,1},{3,2},{5,4},{6,5},{7,6},{9,8},{10,9},{11,10},{13,12},{... | collective-permute-start | bytes 55304 | tf_op jit(solution)/shard_map/ppermute | solution.py:17
  26.8 3.6 %collective-permute-start.2 = (bf16[1,18,1,512]{3,2,1,0:T(2,128)(2,1)}, bf16[1,18,1,512]{3,2,1,0:T(2,128)(2,1)}, u32[]{:S(2)}, u32[]{:S(2)}) collective-permute-start(bf16[1,18,1,512]{3,2,1,0:T(2,128)(2,1)} %get-tuple-element.16), channel_id=1, source_target_pairs={{0,1},{1,2},{2,3},{4,5},{5,6},{6,7},{8,9},{9,10},{10,11},{12,13},{... | collective-permute-start | bytes 55304 | tf_op jit(solution)/shard_map/ppermute | solution.py:16
  30.4 4.9 %gather_fusion = bf16[1024,256]{1,0:T(8,128)(2,1)} fusion(bf16[2048,256]{1,0:T(8,128)(2,1)S(1)} %copy-done.1, s32[1024]{0:T(1024)S(1)} %broadcast_clamp_fusion), kind=kCustom, calls=%fused_computation | custom fusion | bytes 1052672 | tf_op jit(solution)/shard_map/gather | solution.py:56
  35.4 6.9 %all-to-all-start.1 = ((bf16[32,32,256]{2,1,0:T(8,128)(2,1)}), bf16[32,32,256]{2,1,0:T(8,128)(2,1)S(1)}, u32[]{:S(2)}, u32[]{:S(2)}) async-start(bf16[32,32,256]{2,1,0:T(8,128)(2,1)} %bitcast.83), calls=%async_computation.1 | async-start | bytes 1048576 | tf_op jit(solution)/shard_map/all_to_all | solution.py:43
  42.3 1.4 %maximum_bitcast_fusion.1 = bf16[18,1,34,512]{3,2,0,1:T(8,128)(2,1)S(1)} fusion(bf16[1,18,1,512]{3,2,1,0:T(2,128)(2,1)S(1)} %collective-permute-done.3, bf16[1,1,32,512]{3,2,1,0:T(8,128)(2,1)S(1)} %collective-permute-done.1, bf16[1,16,32,512]{3,2,1,0:T(8,128)(2,1)} %bitcast.80, bf16[1,1,32,512]{3,2,1,0:T(8,128)(2,1)S(1)} %collective-permute-done, ...), kind=kLoop, calls=%fused_computation.28 | loop fusion | flops 3133440 | bytes 1253376 | tf_op jit(solution)/shard_map/concatenate | solution.py:18
  44.4 1.7 %copy-done.4 = bf16[3,3,512,512]{3,2,1,0:T(8,128)(2,1)S(1)} copy-done((bf16[3,3,512,512]{3,2,1,0:T(8,128)(2,1)S(1)}, bf16[3,3,512,512]{3,2,1,0:T(8,128)(2,1)}, u32[]{:S(2)}) %copy-start.4) | copy-done | bytes 4718616
  46.1 3.4 %multiply_convert_fusion = bf16[16,8,5,512]{3,1,2,0:T(8,128)(2,1)S(1)} fusion(bf16[3,3,512,512]{3,2,1,0:T(8,128)(2,1)S(1)} %copy-done.4, bf16[18,1,7,2,512]{4,2,3,0,1:T(8,128)(2,1)S(1)} %slice.54, bf16[18,1,8,5,512]{4,2,3,0,1:T(8,128)(2,1)S(1)} %copy.32, f32[512]{0:T(512)S(1)} %copy-done.5, pred[8,5]{0,1:T(8,128)(4,1)S(1)} %copy-done.7), kind=kOutput, calls=%fused_computation.11 | convolution fusion | flops 3025289216 | bytes 6371368 | tf_op jit(solution)/shard_map/conv_general_dilated | solution.py:23
  50.3 0.6 copy.35
  51.0 1.5 %reshape.247 = bf16[1,1,40,512]{3,1,2,0:T(2,128)(2,1)} reshape(bf16[1,8,5,512]{3,2,1,0:T(8,128)(2,1)} %copy.35) | data formatting | bytes 81920 | tf_op jit(solution)/shard_map/convert_element_type | solution.py:48
  52.5 1.5 %slice.59 = bf16[1,1,32,512]{3,1,2,0:T(2,128)(2,1)} slice(bf16[1,1,40,512]{3,1,2,0:T(2,128)(2,1)} %reshape.247), slice={[0:1], [0:1], [0:32], [0:512]} | slice | bytes 65536 | tf_op jit(solution)/shard_map/convert_element_type | solution.py:48
  54.0 1.3 %collective-permute-start.5 = (bf16[1,1,32,512]{3,1,2,0:T(2,128)(2,1)}, bf16[1,1,32,512]{3,1,2,0:T(2,128)(2,1)}, u32[]{:S(2)}, u32[]{:S(2)}) collective-permute-start(bf16[1,1,32,512]{3,1,2,0:T(2,128)(2,1)} %slice.59), channel_id=1, source_target_pairs={{4,0},{8,4},{12,8},{16,12},{20,16},{24,20},{28,24},{5,1},{9,5},{13... | collective-permute-start | bytes 98312 | tf_op jit(solution)/shard_map/ppermute | solution.py:17
  55.3 1.4 %copy.33 = bf16[1,8,5,512]{3,2,1,0:T(8,128)(2,1)} copy(bf16[1,8,5,512]{3,1,2,0:T(8,128)(2,1)} %get-tuple-element.14) | data formatting | bytes 81920 | tf_op jit(solution)/shard_map/convert_element_type | solution.py:48
  56.7 1.5 %reshape.163 = bf16[1,1,40,512]{3,2,1,0:T(8,128)(2,1)} reshape(bf16[1,8,5,512]{3,2,1,0:T(8,128)(2,1)} %copy.33) | data formatting | bytes 81920 | tf_op jit(solution)/shard_map/convert_element_type | solution.py:48
  58.2 0.8 slice.56
  58.9 4.5 %collective-permute-start.4 = (bf16[1,1,32,512]{3,2,1,0:T(8,128)(2,1)S(1)}, bf16[1,1,32,512]{3,2,1,0:T(8,128)(2,1)S(1)}, u32[]{:S(2)}, u32[]{:S(2)}) collective-permute-start(bf16[1,1,32,512]{3,2,1,0:T(8,128)(2,1)S(1)} %slice.56), channel_id=1, source_target_pairs={{0,4},{4,8},{8,12},{12,16},{16,20},{20,24},{24,28},{1,5},{5,9},{9,... | collective-permute-start | bytes 98312 | tf_op jit(solution)/shard_map/ppermute | solution.py:16
  63.5 1.5 %collective-permute-done.4 = bf16[1,1,32,512]{3,2,1,0:T(8,128)(2,1)S(1)} collective-permute-done((bf16[1,1,32,512]{3,2,1,0:T(8,128)(2,1)S(1)}, bf16[1,1,32,512]{3,2,1,0:T(8,128)(2,1)S(1)}, u32[]{:S(2)}, u32[]{:S(2)}) %collective-permute-start.4) | collective-permute-done | bytes 32800 | tf_op jit(solution)/shard_map/ppermute | solution.py:16
  65.1 0.7 pad_maximum_fusion.5
  65.8 1.3 %collective-permute-start.7 = (bf16[1,18,1,512]{3,1,2,0:T(8,128)(2,1)S(1)}, bf16[1,18,1,512]{3,1,2,0:T(8,128)(2,1)S(1)}, u32[]{:S(2)}, u32[]{:S(2)}) collective-permute-start(bf16[1,18,1,512]{3,1,2,0:T(8,128)(2,1)S(1)} %get-tuple-element.13), channel_id=1, source_target_pairs={{1,0},{2,1},{3,2},{5,4},{6,5},{7,6},{9,8},{10,9},{11,10},{13,12},{... | collective-permute-start | bytes 55304 | tf_op jit(solution)/shard_map/ppermute | solution.py:17
  67.1 3.0 %collective-permute-start.6 = (bf16[1,18,1,512]{3,1,2,0:T(8,128)(2,1)S(1)}, bf16[1,18,1,512]{3,1,2,0:T(8,128)(2,1)S(1)}, u32[]{:S(2)}, u32[]{:S(2)}) collective-permute-start(bf16[1,18,1,512]{3,1,2,0:T(8,128)(2,1)S(1)} %get-tuple-element.12), channel_id=1, source_target_pairs={{0,1},{1,2},{2,3},{4,5},{5,6},{6,7},{8,9},{9,10},{10,11},{12,13},{... | collective-permute-start | bytes 55304 | tf_op jit(solution)/shard_map/ppermute | solution.py:16
  70.2 0.8 collective-permute-done.6
  71.0 1.3 %maximum_bitcast_fusion = bf16[18,1,34,512]{3,0,2,1:T(8,128)(2,1)S(1)} fusion(bf16[1,18,1,512]{3,1,2,0:T(8,128)(2,1)S(1)} %collective-permute-done.7, bf16[1,1,32,512]{3,1,2,0:T(2,128)(2,1)} %collective-permute-done.5, bf16[1,16,32,512]{3,1,2,0:T(8,128)(2,1)S(1)} %slice_bitcast_fusion, bf16[1,1,32,512]{3,1,2,0:T(2,128)(2,1)S(1)} %copy.37, ...), kind=kLoop, calls=%fused_computation.27 | loop fusion | flops 3133440 | bytes 1253376 | tf_op jit(solution)/shard_map/concatenate | solution.py:18
  73.0 1.7 %fusion.3 = f32[16,8,5,256]{3,1,2,0:T(8,128)S(1)} fusion(bf16[3,3,512,256]{3,2,1,0:T(8,128)(2,1)S(1)} %copy-done, bf16[18,1,7,2,512]{4,2,3,0,1:T(8,128)(2,1)S(1)} %slice.60, bf16[18,1,8,5,512]{4,2,3,0,1:T(8,128)(2,1)S(1)} %copy.39, f32[256]{0:T(256)S(1)} %copy-done.6, pred[8,5]{0,1:T(8,128)(4,1)S(1)} %copy-done.8), kind=kOutput, calls=%fused_computation.13 | convolution fusion | flops 1513373696 | bytes 4011048 | tf_op jit(solution)/shard_map/conv_general_dilated | solution.py:23
  75.0 1.1 copy.44
  76.1 3.7 %scatter_custom_fusion.1 = f32[1024,256]{1,0:T(8,128)} fusion(s32[512]{0:T(512)} %bitcast.88, f32[512,256]{1,0:T(8,128)} %bitcast.84, f32[]{:T(128)} %constant.14.clone.1), kind=kCustom, calls=%fused_computation.38 | custom fusion | bytes 1049088 | tf_op jit(solution)/shard_map/scatter | solution.py:84
  79.8 2.1 %convert_element_type.69 = bf16[1024,256]{1,0:T(8,128)(2,1)} convert(f32[1024,256]{1,0:T(8,128)} %scatter_custom_fusion.1) | non-fusion elementwise | flops 262144 | bytes 1572864 | tf_op jit(solution)/shard_map/convert_element_type | solution.py:37
  81.9 9.6 %all-to-all-start.2 = ((bf16[32,32,256]{2,1,0:T(8,128)(2,1)}), bf16[32,32,256]{2,1,0:T(8,128)(2,1)}, u32[]{:S(2)}, u32[]{:S(2)}) async-start(bf16[32,32,256]{2,1,0:T(8,128)(2,1)} %bitcast.82), calls=%async_computation.2 | async-start | bytes 1048576 | tf_op jit(solution)/shard_map/all_to_all | solution.py:36
  91.4 1.3 %pad_clamp_fusion = s32[1024]{0:T(1024)} fusion(s32[512]{0:T(512)} %bitcast.89), kind=kLoop, calls=%fused_computation.61 | loop fusion | flops 1024 | bytes 6144 | tf_op jit(solution)/shard_map/gather | solution.py:97
  92.7 0.7 fusion.32
  93.4 0.8 reshape.240
  94.2 6.8 %scatter_custom_fusion.3 = f32[2048]{0:T(1024)} fusion(s32[1024]{0:T(1024)} %copy-done.2, f32[1024]{0:T(1024)S(1)} %reshape.240, f32[]{:T(128)} %constant.14.clone.1), kind=kCustom, calls=%fused_computation.62 | custom fusion | flops 1024 | bytes 8704 | tf_op jit(solution)/shard_map/scatter-add | solution.py:96
  100.9 2.7 %gather_fusion.1 = bf16[512,256]{1,0:T(8,128)(2,1)} fusion(bf16[1024,256]{1,0:T(8,128)(2,1)S(1)} %bitcast.70, s32[1024]{0:T(1024)} %pad_clamp_fusion), kind=kCustom, calls=%fused_computation.1 | custom fusion | bytes 526336 | tf_op jit(solution)/shard_map/gather | solution.py:97
  103.6 1.0 convert_element_type.73
  104.6 1.4 %fusion.22 = bf16[1,1,1,16,32,256]{5,3,4,2,1,0:T(8,128)(2,1)S(1)} fusion(f32[1,1,1,16,32,256]{5,4,3,2,1,0:T(8,128)S(1)} %bitcast.74, bf16[1,1,1,16,32,256]{5,4,3,2,1,0:T(8,128)(2,1)} %param.15, f32[16,1,40,256]{3,0,2,1:T(8,128)S(1)} %bitcast.72), kind=kLoop, calls=%fused_computation.36 | loop fusion | flops 655360 | bytes 1572864 | tf_op jit(solution)/shard_map/convert_element_type | solution.py:102
  106.0 0.8 copy.45
  107.2 7.1 %psum.7 = f32[1,16]{1,0:T(1,128)S(1)} all-reduce(f32[1,16]{1,0:T(1,128)S(1)} %bitcast.91), channel_id=1, replica_groups=mesh['tile'=8,'code'=4] {'code'}, use_global_device_ids=true, to_apply=%region_5.6 | all-reduce | flops 16 | bytes 128 | tf_op jit(solution)/shard_map/psum | solution.py:106
  114.8 8.4 %scatter_custom_fusion.2 = f32[2048,256]{1,0:T(8,128)} fusion(s32[1024]{0:T(1024)} %copy-done.2, bf16[1024,256]{1,0:T(8,128)(2,1)} %bitcast.27, f32[]{:T(128)} %constant.14.clone.1, f32[1024]{0:T(1024)S(1)} %reshape.240), kind=kCustom, calls=%fused_computation.15 | custom fusion | flops 786432 | bytes 2626048 | tf_op jit(solution)/shard_map/scatter-add | solution.py:94
  (46 shorter events, 3.8 us)
Async XLA Ops:
  0.6 72.1 %copy-start = (bf16[3,3,512,256]{3,2,1,0:T(8,128)(2,1)S(1)}, bf16[3,3,512,256]{3,2,1,0:T(8,128)(2,1)}, u32[]{:S(2)}) copy-start(bf16[3,3,512,256]{3,2,1,0:T(8,128)(2,1)} %param.12) | copy-start | bytes 7077892
  0.6 29.8 %copy-start.1 = (bf16[2048,256]{1,0:T(8,128)(2,1)S(1)}, bf16[2048,256]{1,0:T(8,128)(2,1)}, u32[]{:S(2)}) copy-start(bf16[2048,256]{1,0:T(8,128)(2,1)} %param.14) | copy-start | bytes 3145732
  4.4 12.0 %copy-start.3 = (s32[512,1]{0,1:T(1,128)}, s32[512,1]{0,1:T(1,128)S(1)}, u32[]{:S(2)}) copy-start(s32[512,1]{0,1:T(1,128)S(1)} %compare_select_fusion) | copy-start | bytes 6148
  7.7 14.6 %all-to-all-start = ((s32[32,1,32]{2,1,0:T(1,128)}), s32[32,1,32]{2,1,0:T(1,128)S(1)}, u32[]{:S(2)}, u32[]{:S(2)}) async-start(s32[32,1,32]{2,1,0:T(1,128)} %all_to_all.12), calls=%async_computation | async-start | bytes 32768 | tf_op jit(solution)/shard_map/all_to_all | solution.py:35
  16.4 6.0 %collective-permute-start.1 = (bf16[1,1,32,512]{3,2,1,0:T(8,128)(2,1)}, bf16[1,1,32,512]{3,2,1,0:T(8,128)(2,1)S(1)}, u32[]{:S(2)}, u32[]{:S(2)}) collective-permute-start(bf16[1,1,32,512]{3,2,1,0:T(8,128)(2,1)} %get-tuple-element.19), channel_id=1, source_target_pairs={{4,0},{8,4},{12,8},{16,12},{20,16},{24,20},{28,24},{5,1},{9,5},{13... | collective-permute-start | bytes 98312 | tf_op jit(solution)/shard_map/ppermute | solution.py:17
  17.7 6.1 %collective-permute-start = (bf16[1,1,32,512]{3,2,1,0:T(8,128)(2,1)S(1)}, bf16[1,1,32,512]{3,2,1,0:T(8,128)(2,1)S(1)}, u32[]{:S(2)}, u32[]{:S(2)}) collective-permute-start(bf16[1,1,32,512]{3,2,1,0:T(8,128)(2,1)S(1)} %get-tuple-element.18), channel_id=1, source_target_pairs={{0,4},{4,8},{8,12},{12,16},{16,20},{20,24},{24,28},{1,5},{5,9},{9,... | collective-permute-start | bytes 98312 | tf_op jit(solution)/shard_map/ppermute | solution.py:16
  22.4 13.0 %copy-start.2 = (s32[1024]{0:T(1024)}, s32[1024]{0:T(1024)S(1)}, u32[]{:S(2)}) copy-start(s32[1024]{0:T(1024)S(1)} %reshape.198) | copy-start | bytes 12292
  25.5 16.8 %collective-permute-start.3 = (bf16[1,18,1,512]{3,2,1,0:T(2,128)(2,1)}, bf16[1,18,1,512]{3,2,1,0:T(2,128)(2,1)S(1)}, u32[]{:S(2)}, u32[]{:S(2)}) collective-permute-start(bf16[1,18,1,512]{3,2,1,0:T(2,128)(2,1)} %get-tuple-element.17), channel_id=1, source_target_pairs={{1,0},{2,1},{3,2},{5,4},{6,5},{7,6},{9,8},{10,9},{11,10},{13,12},{... | collective-permute-start | bytes 55304 | tf_op jit(solution)/shard_map/ppermute | solution.py:17
  26.8 15.6 %collective-permute-start.2 = (bf16[1,18,1,512]{3,2,1,0:T(2,128)(2,1)}, bf16[1,18,1,512]{3,2,1,0:T(2,128)(2,1)}, u32[]{:S(2)}, u32[]{:S(2)}) collective-permute-start(bf16[1,18,1,512]{3,2,1,0:T(2,128)(2,1)} %get-tuple-element.16), channel_id=1, source_target_pairs={{0,1},{1,2},{2,3},{4,5},{5,6},{6,7},{8,9},{9,10},{10,11},{12,13},{... | collective-permute-start | bytes 55304 | tf_op jit(solution)/shard_map/ppermute | solution.py:16
  35.4 46.5 %all-to-all-start.1 = ((bf16[32,32,256]{2,1,0:T(8,128)(2,1)}), bf16[32,32,256]{2,1,0:T(8,128)(2,1)S(1)}, u32[]{:S(2)}, u32[]{:S(2)}) async-start(bf16[32,32,256]{2,1,0:T(8,128)(2,1)} %bitcast.83), calls=%async_computation.1 | async-start | bytes 1048576 | tf_op jit(solution)/shard_map/all_to_all | solution.py:43
  43.8 2.3 %copy-start.4 = (bf16[3,3,512,512]{3,2,1,0:T(8,128)(2,1)S(1)}, bf16[3,3,512,512]{3,2,1,0:T(8,128)(2,1)}, u32[]{:S(2)}) copy-start(bf16[3,3,512,512]{3,2,1,0:T(8,128)(2,1)} %param.10) | copy-start | bytes 14155780
  44.0 2.1 %copy-start.5 = (f32[512]{0:T(512)S(1)}, f32[512]{0:T(512)}, u32[]{:S(2)}) copy-start(f32[512]{0:T(512)} %param.11) | copy-start | bytes 6148
  44.0 2.1 %copy-start.7 = (pred[8,5]{0,1:T(8,128)(4,1)S(1)}, pred[8,5]{0,1:T(8,128)(4,1)}, u32[]{:S(2)}) copy-start(pred[8,5]{0,1:T(8,128)(4,1)} %constant.43) | copy-start | bytes 124
  54.0 11.1 %collective-permute-start.5 = (bf16[1,1,32,512]{3,1,2,0:T(2,128)(2,1)}, bf16[1,1,32,512]{3,1,2,0:T(2,128)(2,1)}, u32[]{:S(2)}, u32[]{:S(2)}) collective-permute-start(bf16[1,1,32,512]{3,1,2,0:T(2,128)(2,1)} %slice.59), channel_id=1, source_target_pairs={{4,0},{8,4},{12,8},{16,12},{20,16},{24,20},{28,24},{5,1},{9,5},{13... | collective-permute-start | bytes 98312 | tf_op jit(solution)/shard_map/ppermute | solution.py:17
  58.9 6.1 %collective-permute-start.4 = (bf16[1,1,32,512]{3,2,1,0:T(8,128)(2,1)S(1)}, bf16[1,1,32,512]{3,2,1,0:T(8,128)(2,1)S(1)}, u32[]{:S(2)}, u32[]{:S(2)}) collective-permute-start(bf16[1,1,32,512]{3,2,1,0:T(8,128)(2,1)S(1)} %slice.56), channel_id=1, source_target_pairs={{0,4},{4,8},{8,12},{12,16},{16,20},{20,24},{24,28},{1,5},{5,9},{9,... | collective-permute-start | bytes 98312 | tf_op jit(solution)/shard_map/ppermute | solution.py:16
  65.8 4.3 %collective-permute-start.7 = (bf16[1,18,1,512]{3,1,2,0:T(8,128)(2,1)S(1)}, bf16[1,18,1,512]{3,1,2,0:T(8,128)(2,1)S(1)}, u32[]{:S(2)}, u32[]{:S(2)}) collective-permute-start(bf16[1,18,1,512]{3,1,2,0:T(8,128)(2,1)S(1)} %get-tuple-element.13), channel_id=1, source_target_pairs={{1,0},{2,1},{3,2},{5,4},{6,5},{7,6},{9,8},{10,9},{11,10},{13,12},{... | collective-permute-start | bytes 55304 | tf_op jit(solution)/shard_map/ppermute | solution.py:17
  67.1 3.9 %collective-permute-start.6 = (bf16[1,18,1,512]{3,1,2,0:T(8,128)(2,1)S(1)}, bf16[1,18,1,512]{3,1,2,0:T(8,128)(2,1)S(1)}, u32[]{:S(2)}, u32[]{:S(2)}) collective-permute-start(bf16[1,18,1,512]{3,1,2,0:T(8,128)(2,1)S(1)} %get-tuple-element.12), channel_id=1, source_target_pairs={{0,1},{1,2},{2,3},{4,5},{5,6},{6,7},{8,9},{9,10},{10,11},{12,13},{... | collective-permute-start | bytes 55304 | tf_op jit(solution)/shard_map/ppermute | solution.py:16
  72.3 0.7 copy-start.6
  72.3 0.7 copy-start.8
  81.9 32.9 %all-to-all-start.2 = ((bf16[32,32,256]{2,1,0:T(8,128)(2,1)}), bf16[32,32,256]{2,1,0:T(8,128)(2,1)}, u32[]{:S(2)}, u32[]{:S(2)}) async-start(bf16[32,32,256]{2,1,0:T(8,128)(2,1)} %bitcast.82), calls=%async_computation.2 | async-start | bytes 1048576 | tf_op jit(solution)/shard_map/all_to_all | solution.py:36
where the time goes:
time: 125 us; the launch traced here: 123 us
  starting transfers between devices  44.7 us (36%)
  other arithmetic  31.1 us (25%)
  local copies, waits for them, and re-layouts  30.5 us (24%)
  blocking collectives  7.07 us (6%)
  matrix products  5.08 us (4%)
  waiting for transfers between devices  3.81 us (3%)
    ppermute x4, starting transfers between devices, extended(): before = lax.ppermute(last, axis, up)  15.8 us
    all_to_all x1, starting transfers between devices, send_joint(): lax.all_to_all(parcel.astype(jnp.bfloat16), ('tile', 'code'), split_axis=...  9.55 us
    scatter-add x1, other arithmetic, shards(): code_sums = jnp.zeros((codebook.shape[0], latent_width), jnp.float32).at[...  8.37 us
    convert_element_type x9, local copies, waits for them, and re-layouts, compute_latent(): jax.nn.silu(convolve(padded, w_first) + b_first).astype(jnp.bfloat16)  8.19 us
    all_to_all x1, starting transfers between devices, send_joint(): lax.all_to_all(requests, ('tile', 'code'), split_axis=0, concat_axis=0, t...  7.3 us
    psum x1, blocking collectives, shards(): total = lax.psum(squared, 'code')  7.07 us
    all_to_all x1, starting transfers between devices, send_back(): lax.all_to_all(answer, ('tile', 'code'), split_axis=0, concat_axis=0, til...  6.94 us
    scatter-add x1, other arithmetic, shards(): jnp.zeros((codebook.shape[0],), jnp.float32).at[safe_index].add(weights)  6.75 us
  transfers between devices with their start and end apart: 11, of which 3 were waited for; matrix products, arithmetic and copies ran while one was open for 39% of the time, Pallas kernels for 0%

commit v1 on v0

v1 whole, which is shorter than its diff:
```python
import functools

import jax
import jax.numpy as jnp
from jax import lax
from jax.experimental import pallas as pl
from jax.experimental.pallas import tpu as pltpu
from jax.sharding import PartitionSpec as P

BETA = 0.25
BF, F32, I32 = jnp.bfloat16, jnp.float32, jnp.int32
MESH = pl.DeviceIdType.MESH
LANES = 128


def iota(shape, dim):
    return lax.broadcasted_iota(I32, shape, dim)


def dot(a, b):
    return jnp.dot(a, b, preferred_element_type=F32)


def body(
    tiles, cols_of, rows, cols, cap,
    x_ref, w1_hbm, b1_ref, w2_hbm, b2_ref, book_hbm, up_hbm, own_ref, loc_ref,
    grad_ref, loss_ref, sums_ref, counts_ref,
    w1, w2, book, up, pack, top, bot, side, corner, colbuf, im1, hid, im2,
    req_out, req_in, onehot, onehot_t, pick, pick_t, ans, ret, par, arr, loss_out, loss_in,
    local_sem, halo_send, halo_recv, send_sem, recv_sem,
):
    n = tiles * cols_of
    tok = rows * cols
    width = x_ref.shape[1]
    codes = book.shape[0]
    slots = n * cap
    groups = slots // LANES
    per = LANES // cap
    shift = cols.bit_length() - 1
    a, b = lax.axis_index("tile"), lax.axis_index("code")
    me = a * cols_of + b

    loads = []
    for i, (src, dst) in enumerate(((book_hbm, book), (w1_hbm, w1), (w2_hbm, w2), (up_hbm, up))):
        copy = pltpu.make_async_copy(src, dst, local_sem.at[i])
        copy.start()
        loads.append(copy)

    def place_of(i):
        d = lax.rem(me + i, n)
        return d, (d // cols_of, lax.rem(d, cols_of))

    barrier = pltpu.get_barrier_semaphore()

    def greet(i, _):
        pl.semaphore_signal(barrier, inc=1, device_id=place_of(i)[1], device_id_type=MESH)
        return 0

    lax.fori_loop(1, n, greet, 0)

    o = iota((128, tok), 0)
    t = iota((128, tok), 1)
    col_row, col_col = o & 15, ((o >> 4) & 1) + (o >> 5) * (cols - 2)
    k, q = o & 15, (o >> 4) & 3
    cor_row = (k >> 1) + (q >> 1) * (rows - 2)
    cor_col = (k & 1) + (q & 1) * (cols - 2)
    from_col = (o < 64) & (t == col_row * cols + col_col)
    from_cor = (o >= 64) & (k < 4) & (t == cor_row * cols + cor_col)
    pack[...] = dot(jnp.where(from_col | from_cor, 1.0, 0.0).astype(BF), x_ref[...]).astype(BF)

    own = own_ref[...]
    loc = loc_ref[...]
    member = jnp.where(iota((n, tok), 0) == own, 1.0, 0.0)
    before = jnp.where(iota((tok, tok), 0) < iota((tok, tok), 1), 1.0, 0.0).astype(BF)
    earlier = dot(member.astype(BF), before)
    rank = jnp.sum(member * earlier, axis=0, keepdims=True)
    place = own.astype(F32) * cap + rank
    r8 = iota((8, tok), 0)
    stack = jnp.where(r8 == 0, rank, jnp.where(r8 == 1, loc.astype(F32), place))
    columns = jnp.transpose(stack)
    rank_c, loc_c, place_c = columns[:, 0:1], columns[:, 1:2], columns[:, 2:3]
    high = jnp.floor(loc_c * (1.0 / 64.0))
    low = loc_c - high * 64.0 + 1.0
    lane = iota((tok, LANES), 1).astype(F32)
    seat = lane == rank_c + (lax.rem(me, per) * cap).astype(F32)
    asked_high = dot(member.astype(BF), jnp.where(seat, high, 0.0).astype(BF))
    asked_low = dot(member.astype(BF), jnp.where(seat, low, 0.0).astype(BF))
    wanted = asked_high * 64.0 + asked_low
    for d in range(n):
        req_out[d] = jnp.broadcast_to(wanted[d : d + 1, :], (8, LANES))
    req_in[me] = req_out[me]

    up_ok, down_ok = a > 0, a < tiles - 1
    left_ok, right_ok = b > 0, b < cols_of - 1
    hops = (
        (up_ok, -1, 0), (down_ok, 1, 0), (left_ok, 0, -1), (right_ok, 0, 1),
        (up_ok & left_ok, -1, -1), (up_ok & right_ok, -1, 1),
        (down_ok & left_ok, 1, -1), (down_ok & right_ok, 1, 1),
    )
    edge = 2 * cols
    outgoing = (
        x_ref.at[pl.ds(0, edge)], x_ref.at[pl.ds(tok - edge, edge)],
        pack.at[pl.ds(0, 32)], pack.at[pl.ds(32, 32)],
        pack.at[pl.ds(64, 16)], pack.at[pl.ds(80, 16)],
        pack.at[pl.ds(96, 16)], pack.at[pl.ds(112, 16)],
    )
    landing = (top, bot, side.at[0], side.at[1], corner.at[0], corner.at[1], corner.at[2], corner.at[3])
    opposite = (1, 0, 3, 2, 7, 6, 5, 4)

    def halo(i):
        _, da, db = hops[i]
        return pltpu.make_async_remote_copy(
            src_ref=outgoing[i], dst_ref=landing[opposite[i]],
            send_sem=halo_send.at[i], recv_sem=halo_recv.at[opposite[i]],
            device_id=(a + da, b + db), device_id_type=MESH,
        )

    def arrival(i):
        return pltpu.make_async_copy(landing[i], landing[i], halo_recv.at[i])

    pl.semaphore_wait(barrier, n - 1)

    def send_all(src, dst, phase, rows_each):
        def step(i, _):
            d, where = place_of(i)
            if rows_each is None:
                s, r = src.at[d], dst.at[me]
            else:
                s = src.at[pl.ds(pl.multiple_of(d * rows_each, rows_each), rows_each)]
                r = dst.at[pl.ds(pl.multiple_of(me * rows_each, rows_each), rows_each)]
            pltpu.make_async_remote_copy(
                src_ref=s, dst_ref=r, send_sem=send_sem.at[phase], recv_sem=recv_sem.at[phase],
                device_id=where, device_id_type=MESH,
            ).start()
            return 0

        lax.fori_loop(1, n, step, 0)

    def wait_all(buf, sem, rows_each):
        part = buf.at[pl.ds(0, (n - 1) * (1 if rows_each is None else rows_each))]
        pltpu.make_async_copy(part, part, sem).wait()

    send_all(req_out, req_in, 0, None)
    for i in range(8):
        pl.when(hops[i][0])(lambda i=i: halo(i).start())

        @pl.when(jnp.logical_not(hops[i][0]))
        def _(i=i):
            landing[i][...] = jnp.zeros(landing[i].shape, BF)

    pick[...] = jnp.where(iota((slots, tok), 0).astype(F32) == place, 1.0, 0.0).astype(BF)
    pick_t[...] = jnp.where(iota((tok, slots), 1).astype(F32) == place_c, 1.0, 0.0).astype(BF)

    loads[0].wait()
    wait_all(req_in, recv_sem.at[0], None)
    sub8 = iota((8, LANES), 0)
    asked = []
    for g in range(groups):
        total = req_in[g * per]
        for j in range(1, per):
            total = total + req_in[g * per + j]
        asked.append(total)
    for g8 in range(groups // 8):
        table = jnp.zeros((8, LANES), F32)
        for g in range(8):
            table = jnp.where(sub8 == g, asked[g8 * 8 + g], table)
        table = jnp.transpose(table)
        for g in range(8):
            first = (g8 * 8 + g) * LANES
            hot = iota((LANES, codes), 1).astype(F32) + 1.0 == table[:, g : g + 1]
            onehot[pl.ds(first, LANES), :] = jnp.where(hot, 1.0, 0.0).astype(BF)
    ans[...] = dot(onehot[...], book[...]).astype(BF)
    mine = pl.ds(pl.multiple_of(me * cap, cap), cap)
    ret[mine, :] = ans[mine, :]
    send_all(ans, ret, 1, cap)

    for i in range(8):
        pl.when(hops[i][0])(lambda i=i: arrival(i).wait())
    for s in range(2):
        for c in range(2):
            slot = (0, 1, 4, 5)[s * 2 + c]
            colbuf[slot, 8:24, :] = side[s, c * 16 : c * 16 + 16, :].astype(F32)
        slot = 2 + s
        edge_col = s * (cols - 1)
        colbuf[slot, 8:24, :] = pack[s * 48 : s * 48 + 16, :].astype(F32)
        tf, bf_ = top[...].astype(F32), bot[...].astype(F32)
        for r in range(2):
            at = r * cols + edge_col
            colbuf[slot, 6 + r : 7 + r, :] = tf[at : at + 1, :]
            colbuf[slot, 24 + r : 25 + r, :] = bf_[at : at + 1, :]
    for q in range(4):
        piece = corner[q].astype(F32)
        for r in range(2):
            for c in range(2):
                slot = (0, 1, 4, 5)[(q % 2) * 2 + c]
                at = (6 if q < 2 else 24) + r
                colbuf[slot, at : at + 1, :] = piece[r * 2 + c : r * 2 + c + 1, :]
    for slot in range(6):
        colbuf[slot, 26:32, :] = jnp.zeros((6, width), F32)
    sub = iota((cols, width), 0)

    def spread(buf, count, r, three):
        for dx in range(3):
            for dy in range(3):
                if 0 <= r - dy < count:
                    buf[(r - dy) * cols : (r - dy + 1) * cols, (dy * 3 + dx) * width : (dy * 3 + dx + 1) * width] = three[dx]

    def shifted(row, before_col, after_col):
        left = jnp.where(sub == 0, before_col, pltpu.roll(row, 1, 0))
        right = jnp.where(sub == cols - 1, after_col, pltpu.roll(row, cols - 1, 0))
        return left.astype(BF), row.astype(BF), right.astype(BF)

    for r in range(rows + 4):
        if r < 2:
            row = top[r * cols : (r + 1) * cols, :]
        elif r < rows + 2:
            row = x_ref[(r - 2) * cols : (r - 1) * cols, :]
        else:
            row = bot[(r - rows - 2) * cols : (r - rows - 1) * cols, :]
        three = shifted(row.astype(F32), colbuf[1, 6 + r : 7 + r, :], colbuf[4, 6 + r : 7 + r, :])
        spread(im1, rows + 2, r, three)
    main = (rows + 2) * cols
    for dy in range(3):
        for dx in range(3):
            both = jnp.concatenate(
                [colbuf[dx, 6 + dy : 30 + dy, :], colbuf[3 + dx, 6 + dy : 30 + dy, :]], axis=0
            )
            im1[main : main + 48, (dy * 3 + dx) * width : (dy * 3 + dx + 1) * width] = both.astype(BF)
    loads[1].wait()
    value = dot(im1[...], w1[...]) + b1_ref[...]
    hid[...] = value / (1.0 + jnp.exp(-value))

    tall = [jnp.where(ok, 1.0, 0.0).astype(F32) for ok in (up_ok, down_ok, left_ok, right_ok)]
    for r in range(rows + 2):
        row = hid[r * cols : (r + 1) * cols, :]
        before_col = hid[main + r : main + r + 1, :] * tall[2]
        after_col = hid[main + 24 + r : main + 25 + r, :] * tall[3]
        if r in (0, rows + 1):
            f = tall[0 if r == 0 else 1]
            row, before_col, after_col = row * f, before_col * f, after_col * f
        spread(im2, rows, r, shifted(row, before_col, after_col))
    loads[2].wait()
    latent = dot(im2[...], w2[...]) + b2_ref[...]
    par[...] = dot(pick[...], latent.astype(BF)).astype(BF)
    arr[mine, :] = par[mine, :]
    send_all(par, arr, 2, cap)

    loads[3].wait()
    for g in range(groups):
        hot = (iota((codes, LANES), 0).astype(F32) + 1.0) == asked[g][0:1, :]
        onehot_t[:, g * LANES : (g + 1) * LANES] = jnp.where(hot, 1.0, 0.0).astype(BF)
    counts_ref[...] = dot(jnp.ones((8, slots), BF), onehot[...])[0:1, :]
    wait_all(ret, recv_sem.at[1], cap)
    chosen = dot(pick_t[...], ret[...])
    differ = latent - chosen
    grad_ref[...] = (up[...].astype(F32) + 2.0 * BETA * differ).astype(BF)
    square = differ * differ
    half = square[:, 0:LANES]
    for j in range(1, square.shape[1] // LANES):
        half = half + square[:, j * LANES : (j + 1) * LANES]
    part = jnp.sum(half.reshape(rows, cols, LANES), axis=1)
    loss_out[...] = part
    loss_in[b] = part

    def loss_copy(i):
        peer = lax.rem(b + i, cols_of)
        return pltpu.make_async_remote_copy(
            src_ref=loss_out, dst_ref=loss_in.at[b], send_sem=send_sem.at[3], recv_sem=recv_sem.at[3],
            device_id=(a, peer), device_id_type=MESH,
        )

    for i in range(1, cols_of):
        loss_copy(i).start()

    wait_all(arr, recv_sem.at[2], cap)
    sums_ref[...] = dot(onehot_t[...], arr[...])
    others = loss_in.at[pl.ds(0, cols_of - 1)]
    pltpu.make_async_copy(others, others, recv_sem.at[3]).wait()
    total = loss_in[0]
    for i in range(1, cols_of):
        total = total + loss_in[i]
    line = jnp.sum(jnp.transpose(total), axis=0, keepdims=True)
    loss_ref[...] = BETA * line / (cols * cols_of * square.shape[1])

    pltpu.make_async_copy(others, others, send_sem.at[3]).wait()
    wait_all(req_out, send_sem.at[0], None)
    wait_all(ans, send_sem.at[1], cap)
    wait_all(par, send_sem.at[2], cap)
    for i in range(8):
        pl.when(hops[i][0])(lambda i=i: halo(i).wait_send())


def shards(features, w_first, b_first, w_latent, b_latent, codebook, upstream, owner, local_code):
    tiles, cols_of = lax.axis_size("tile"), lax.axis_size("code")
    n = tiles * cols_of
    rows, cols, width = features.shape[3:]
    tok, latent = rows * cols, w_latent.shape[3]
    codes = codebook.shape[0]
    cap = max(16, 2 * tok // n)
    slots = n * cap
    deep = 9 * width
    vmem = pl.BlockSpec(memory_space=pltpu.VMEM)
    anyw = pl.BlockSpec(memory_space=pl.ANY)
    grad, loss, sums, counts = pl.pallas_call(
        functools.partial(body, tiles, cols_of, rows, cols, cap),
        out_shape=(
            jax.ShapeDtypeStruct((tok, latent), BF),
            jax.ShapeDtypeStruct((1, rows), F32),
            jax.ShapeDtypeStruct((codes, latent), F32),
            jax.ShapeDtypeStruct((1, codes), F32),
        ),
        in_specs=[vmem, anyw, vmem, anyw, vmem, anyw, anyw, vmem, vmem],
        out_specs=(vmem, vmem, vmem, vmem),
        scratch_shapes=[
            pltpu.VMEM((deep, width), BF),
            pltpu.VMEM((deep, latent), BF),
            pltpu.VMEM((codes, latent), BF),
            pltpu.VMEM((tok, latent), BF),
            pltpu.VMEM((128, width), BF),
            pltpu.VMEM((2 * cols, width), BF),
            pltpu.VMEM((2 * cols, width), BF),
            pltpu.VMEM((2, 32, width), BF),
            pltpu.VMEM((4, 16, width), BF),
            pltpu.VMEM((6, 32, width), F32),
            pltpu.VMEM(((rows + 2) * cols + 48, deep), BF),
            pltpu.VMEM(((rows + 2) * cols + 48, width), F32),
            pltpu.VMEM((tok, deep), BF),
            pltpu.VMEM((n, 8, LANES), F32),
            pltpu.VMEM((n, 8, LANES), F32),
            pltpu.VMEM((slots, codes), BF),
            pltpu.VMEM((codes, slots), BF),
            pltpu.VMEM((slots, tok), BF),
            pltpu.VMEM((tok, slots), BF),
            pltpu.VMEM((slots, latent), BF),
            pltpu.VMEM((slots, latent), BF),
            pltpu.VMEM((slots, latent), BF),
            pltpu.VMEM((slots, latent), BF),
            pltpu.VMEM((rows, LANES), F32),
            pltpu.VMEM((cols_of, rows, LANES), F32),
            pltpu.SemaphoreType.DMA((4,)),
            pltpu.SemaphoreType.DMA((8,)),
            pltpu.SemaphoreType.DMA((8,)),
            pltpu.SemaphoreType.DMA((4,)),
            pltpu.SemaphoreType.DMA((4,)),
        ],
        compiler_params=pltpu.CompilerParams(
            collective_id=0, has_side_effects=True, vmem_limit_bytes=60 * 1024 * 1024
        ),
        name="quantize",
    )(
        features.reshape(tok, width),
        w_first.reshape(deep, width),
        b_first.reshape(1, width),
        w_latent.reshape(deep, latent),
        b_latent.reshape(1, latent),
        codebook,
        upstream.reshape(tok, latent),
        owner.reshape(1, tok),
        local_code.reshape(1, tok),
    )
    return grad.reshape(upstream.shape), loss, sums, counts.reshape(codes)


def solution(mesh):
    in_specs = (
        P("tile", "code", None, None, None, None),
        P(),
        P(),
        P(),
        P(),
        P(("tile", "code"), None),
        P("tile", "code", None, None, None, None),
        P("tile", "code", None, None),
        P("tile", "code", None),
    )
    out_specs = (
        P("tile", "code", None, None, None, None),
        P(None, "tile"),
        P(("tile", "code"), None),
        P(("tile", "code")),
    )
    return jax.shard_map(shards, mesh=mesh, in_specs=in_specs, out_specs=out_specs, check_vma=False)
```

time: 125 us -> 49.2 us (0.39)
  the two profiles are of different devices: /device:TPU:0 before, /device:TPU:9 now
where the time goes in v1:
time: 49.2 us; the launch traced here: 48.8 us
  Pallas kernels  41.7 us (85%)
  local copies, waits for them, and re-layouts  6.43 us (13%)
  between operations  0.65 us (1%)
    pallas_call x1, Pallas kernels, shards(): pl.pallas_call(functools.partial(body, tiles, cols_of, rows, cols, cap),...  41.7 us
    unnamed x6, local copies, waits for them, and re-layouts  6.43 us

profile of v1, /device:TPU:9, one launch (start us, length us, event | category | flops | bytes accessed | tf_op | source)
XLA Modules:
  0.0 48.8 jit_solution(11049624652732718936)
XLA Ops:
  0.6 41.7 %quantize.1 = (bf16[512,256]{1,0:T(8,128)(2,1)}, f32[1,16]{1,0:T(1,128)}, f32[2048,256]{1,0:T(8,128)}, f32[1,2048]{1,0:T(1,128)}) custom-call(bf16[512,512]{1,0:T(8,128)(2,1)} %bitcast.12, bf16[4608,512]{1,0:T(8,128)(2,1)} %bitcast.10, f32[1,512]{1,0:T(1,128)} %bitcast.16, bf16[4608,256]{1,0:T(8,128)(2,1)} %bitcast.11, f32[1,256]{1,0:T(1,128)} %bitcast.19, ...), custom_call_target="tpu_custom_call" | custom-call | tf_op jit(solution)/shard_map/quantize/pallas_call | solution.py:304
  42.3 0.0 copy-start
  42.4 1.7 %copy.17 = bf16[1,1,1,16,32,256]{5,4,3,2,1,0:T(8,128)(2,1)} copy(bf16[1,1,1,16,32,256]{5,4,3,2,1,0:T(8,128)(2,1)} %bitcast.14) | data formatting | bytes 524288
  44.0 1.1 %copy.18 = f32[1,16]{1,0:T(1,128)} copy(f32[1,16]{1,0:T(1,128)} %get-tuple-element.17) | data formatting | bytes 128
  45.1 3.0 %copy.19 = f32[2048,256]{1,0:T(8,128)} copy(f32[2048,256]{1,0:T(8,128)} %get-tuple-element.18) | data formatting | bytes 4194304
  48.2 0.0 copy-done
  48.2 0.6 %copy.20 = f32[2048]{0:T(1024)} copy(f32[2048]{0:T(1024)S(1)} %bitcast.15) | data formatting | bytes 16384
Async XLA Ops:
  42.3 5.8 %copy-start = (f32[1,2048]{1,0:T(1,128)S(1)}, f32[1,2048]{1,0:T(1,128)}, u32[]{:S(2)}) copy-start(f32[1,2048]{1,0:T(1,128)} %get-tuple-element.11) | copy-start | bytes 24580

commit v2 on v1

--- a/solution.py
+++ b/solution.py
@@ -1,4 +1,5 @@
 import functools
+import math
 
 import jax
 import jax.numpy as jnp
@@ -24,9 +25,9 @@
 def body(
     tiles, cols_of, rows, cols, cap,
     x_ref, w1_hbm, b1_ref, w2_hbm, b2_ref, book_hbm, up_hbm, own_ref, loc_ref,
-    grad_ref, loss_ref, sums_ref, counts_ref,
+    grad_ref, loss_ref, counts_ref, asked_ref, arr,
     w1, w2, book, up, pack, top, bot, side, corner, colbuf, im1, hid, im2,
-    req_out, req_in, onehot, onehot_t, pick, pick_t, ans, ret, par, arr, loss_out, loss_in,
+    req_out, req_in, onehot, pick, pick_t, ans, ret, par, loss_out, loss_in,
     local_sem, halo_send, halo_recv, send_sem, recv_sem,
 ):
     n = tiles * cols_of
@@ -36,7 +37,7 @@
     slots = n * cap
     groups = slots // LANES
     per = LANES // cap
-    shift = cols.bit_length() - 1
+    hop = next(h for h in range(2 * n // 5, n) if math.gcd(h, n) == 1)
     a, b = lax.axis_index("tile"), lax.axis_index("code")
     me = a * cols_of + b
 
@@ -47,7 +48,7 @@
         loads.append(copy)
 
     def place_of(i):
-        d = lax.rem(me + i, n)
+        d = jnp.bitwise_xor(me, i)
         return d, (d // cols_of, lax.rem(d, cols_of))
 
     barrier = pltpu.get_barrier_semaphore()
@@ -153,26 +154,35 @@
 
     loads[0].wait()
     wait_all(req_in, recv_sem.at[0], None)
-    sub8 = iota((8, LANES), 0)
-    asked = []
-    for g in range(groups):
-        total = req_in[g * per]
+    own_group = me // per
+    code_lane = iota((LANES, codes), 1).astype(F32) + 1.0
+
+    def answer(g, _):
+        group = jnp.bitwise_xor(own_group, groups - 1 - g)
+        total = req_in[group * per]
         for j in range(1, per):
-            total = total + req_in[g * per + j]
-        asked.append(total)
-    for g8 in range(groups // 8):
-        table = jnp.zeros((8, LANES), F32)
-        for g in range(8):
-            table = jnp.where(sub8 == g, asked[g8 * 8 + g], table)
-        table = jnp.transpose(table)
-        for g in range(8):
-            first = (g8 * 8 + g) * LANES
-            hot = iota((LANES, codes), 1).astype(F32) + 1.0 == table[:, g : g + 1]
-            onehot[pl.ds(first, LANES), :] = jnp.where(hot, 1.0, 0.0).astype(BF)
-    ans[...] = dot(onehot[...], book[...]).astype(BF)
+            total = total + req_in[group * per + j]
+        asked_ref[group] = total
+        here = pl.ds(pl.multiple_of(group * LANES, LANES), LANES)
+        hot = jnp.where(code_lane == jnp.transpose(total)[:, 0:1], 1.0, 0.0).astype(BF)
+        onehot[here, :] = hot
+        ans[here, :] = dot(hot, book[...]).astype(BF)
+        for j in range(per):
+            d = group * per + j
+
+            @pl.when(d != me)
+            def _():
+                pltpu.make_async_remote_copy(
+                    src_ref=ans.at[pl.ds(pl.multiple_of(d * cap, cap), cap)],
+                    dst_ref=ret.at[pl.ds(pl.multiple_of(me * cap, cap), cap)],
+                    send_sem=send_sem.at[1], recv_sem=recv_sem.at[1],
+                    device_id=(d // cols_of, lax.rem(d, cols_of)), device_id_type=MESH,
+                ).start()
+        return 0
+
+    lax.fori_loop(0, groups, answer, 0)
     mine = pl.ds(pl.multiple_of(me * cap, cap), cap)
     ret[mine, :] = ans[mine, :]
-    send_all(ans, ret, 1, cap)
 
     for i in range(8):
         pl.when(hops[i][0])(lambda i=i: arrival(i).wait())
@@ -246,9 +256,6 @@
     send_all(par, arr, 2, cap)
 
     loads[3].wait()
-    for g in range(groups):
-        hot = (iota((codes, LANES), 0).astype(F32) + 1.0) == asked[g][0:1, :]
-        onehot_t[:, g * LANES : (g + 1) * LANES] = jnp.where(hot, 1.0, 0.0).astype(BF)
     counts_ref[...] = dot(jnp.ones((8, slots), BF), onehot[...])[0:1, :]
     wait_all(ret, recv_sem.at[1], cap)
     chosen = dot(pick_t[...], ret[...])
@@ -273,7 +280,6 @@
         loss_copy(i).start()
 
     wait_all(arr, recv_sem.at[2], cap)
-    sums_ref[...] = dot(onehot_t[...], arr[...])
     others = loss_in.at[pl.ds(0, cols_of - 1)]
     pltpu.make_async_copy(others, others, recv_sem.at[3]).wait()
     total = loss_in[0]
@@ -288,6 +294,18 @@
     wait_all(par, send_sem.at[2], cap)
     for i in range(8):
         pl.when(hops[i][0])(lambda i=i: halo(i).wait_send())
+
+
+def sum_body(asked, arrived, grad_in, loss_in, counts_in, grad, loss, sums, counts, hot):
+    part = hot.shape[0]
+    code = (iota((part, LANES), 0) + pl.program_id(0) * part + 1).astype(F32)
+    for g in range(asked.shape[0]):
+        same = code == asked[g, 0:1, :]
+        hot[:, g * LANES : (g + 1) * LANES] = jnp.where(same, 1.0, 0.0).astype(BF)
+    sums[...] = dot(hot[...], arrived[...])
+    grad[...] = grad_in[...]
+    loss[...] = loss_in[...]
+    counts[...] = counts_in[...]
 
 
 def shards(features, w_first, b_first, w_latent, b_latent, codebook, upstream, owner, local_code):
@@ -301,16 +319,18 @@
     deep = 9 * width
     vmem = pl.BlockSpec(memory_space=pltpu.VMEM)
     anyw = pl.BlockSpec(memory_space=pl.ANY)
-    grad, loss, sums, counts = pl.pallas_call(
+    groups = slots // LANES
+    grad, loss, counts, asked, arrived = pl.pallas_call(
         functools.partial(body, tiles, cols_of, rows, cols, cap),
         out_shape=(
             jax.ShapeDtypeStruct((tok, latent), BF),
             jax.ShapeDtypeStruct((1, rows), F32),
-            jax.ShapeDtypeStruct((codes, latent), F32),
             jax.ShapeDtypeStruct((1, codes), F32),
+            jax.ShapeDtypeStruct((groups, 8, LANES), F32),
+            jax.ShapeDtypeStruct((slots, latent), BF),
         ),
         in_specs=[vmem, anyw, vmem, anyw, vmem, anyw, anyw, vmem, vmem],
-        out_specs=(vmem, vmem, vmem, vmem),
+        out_specs=(vmem, vmem, vmem, vmem, vmem),
         scratch_shapes=[
             pltpu.VMEM((deep, width), BF),
             pltpu.VMEM((deep, latent), BF),
@@ -328,10 +348,8 @@
             pltpu.VMEM((n, 8, LANES), F32),
             pltpu.VMEM((n, 8, LANES), F32),
             pltpu.VMEM((slots, codes), BF),
-            pltpu.VMEM((codes, slots), BF),
             pltpu.VMEM((slots, tok), BF),
             pltpu.VMEM((tok, slots), BF),
-            pltpu.VMEM((slots, latent), BF),
             pltpu.VMEM((slots, latent), BF),
             pltpu.VMEM((slots, latent), BF),
             pltpu.VMEM((slots, latent), BF),
@@ -358,6 +376,30 @@
         owner.reshape(1, tok),
         local_code.reshape(1, tok),
     )
+    steps = 4
+    part, few = codes // steps, tok // steps
+    still = lambda shape: pl.BlockSpec(shape, lambda i: (0,) * len(shape))
+    grad_spec = pl.BlockSpec((few, latent), lambda i: (i, 0))
+    counts_spec = pl.BlockSpec((1, part), lambda i: (0, i))
+    grad, loss, sums, counts = pl.pallas_call(
+        sum_body,
+        grid=(steps,),
+        out_shape=(
+            jax.ShapeDtypeStruct((tok, latent), BF),
+            jax.ShapeDtypeStruct((1, rows), F32),
+            jax.ShapeDtypeStruct((codes, latent), F32),
+            jax.ShapeDtypeStruct((1, codes), F32),
+        ),
+        in_specs=[
+            still((groups, 8, LANES)), still((slots, latent)), grad_spec, still((1, rows)), counts_spec,
+        ],
+        out_specs=(
+            grad_spec, still((1, rows)), pl.BlockSpec((part, latent), lambda i: (i, 0)), counts_spec,
+        ),
+        scratch_shapes=[pltpu.VMEM((part, slots), BF)],
+        compiler_params=pltpu.CompilerParams(vmem_limit_bytes=60 * 1024 * 1024),
+        name="code_sums",
+    )(asked, arrived, grad, loss, counts)
     return grad.reshape(upstream.shape), loss, sums, counts.reshape(codes)
 
 

time: 49.2 us -> 44.2 us (0.90)
  local copies, waits for them, and re-layouts: 6.43 us -> 0 us
  Pallas kernels: 41.7 us -> 43.3 us
    unnamed x6 -> x0, local copies, waits for them, and re-layouts: 6.43 us -> none
    pallas_call x0 -> x1, Pallas kernels: none -> 4.61 us  [shards(): pl.pallas_call(sum_body, grid=(steps,), out_shape=(jax.ShapeDtypeStruct((...]
    pallas_call x1, Pallas kernels: 41.7 us -> 38.7 us  [shards(): pl.pallas_call(functools.partial(body, tiles, cols_of, rows, cols, cap),...]
where the time goes in v2:
time: 44.2 us; the launch traced here: 43.9 us
  Pallas kernels  43.3 us (98%)
  between operations  0.64 us (1%)
    pallas_call x1, Pallas kernels, shards(): pl.pallas_call(functools.partial(body, tiles, cols_of, rows, cols, cap),...  38.7 us
    pallas_call x1, Pallas kernels, shards(): pl.pallas_call(sum_body, grid=(steps,), out_shape=(jax.ShapeDtypeStruct((...  4.61 us

profile of v2, /device:TPU:9, one launch (start us, length us, event | category | flops | bytes accessed | tf_op | source)
XLA Modules:
  0.0 43.9 jit_solution(5119368727543908679)
XLA Ops:
  0.6 38.7 %quantize.1 = (bf16[512,256]{1,0:T(8,128)(2,1)}, f32[1,16]{1,0:T(1,128)}, f32[1,2048]{1,0:T(1,128)}, f32[8,8,128]{2,1,0:T(8,128)}, bf16[1024,256]{1,0:T(8,128)(2,1)}) custom-call(bf16[512,512]{1,0:T(8,128)(2,1)} %bitcast.12, bf16[4608,512]{1,0:T(8,128)(2,1)} %bitcast.10, f32[1,512]{1,0:T(1,128)} %bitcast.14, bf16[4608,256]{1,0:T(8,128)(2,1)} %bitcast.11, ...), custom_call_target="tpu_custom_call" | custom-call | tf_op jit(solution)/shard_map/quantize/pallas_call | solution.py:323
  39.3 4.6 %code_sums.1 = (bf16[512,256]{1,0:T(8,128)(2,1)}, f32[1,16]{1,0:T(1,128)}, f32[2048,256]{1,0:T(8,128)}, f32[1,2048]{1,0:T(1,128)}) custom-call(f32[8,8,128]{2,1,0:T(8,128)} %get-tuple-element.13.asked, bf16[1024,256]{1,0:T(8,128)(2,1)} %get-tuple-element.14.arrived, bf16[512,256]{1,0:T(8,128)(2,1)} %get-tuple-element.15.grad_in, ...), custom_call_target="tpu_custom_call" | custom-call | tf_op jit(solution)/shard_map/code_sums/pallas_call | solution.py:384

commit v3 on v2

--- a/solution.py
+++ b/solution.py
@@ -376,7 +376,7 @@
         owner.reshape(1, tok),
         local_code.reshape(1, tok),
     )
-    steps = 4
+    steps = 2
     part, few = codes // steps, tok // steps
     still = lambda shape: pl.BlockSpec(shape, lambda i: (0,) * len(shape))
     grad_spec = pl.BlockSpec((few, latent), lambda i: (i, 0))

time: 44.2 us -> 43.4 us (0.982)
  Pallas kernels: 43.3 us -> 42.6 us
    pallas_call x1, Pallas kernels: 4.61 us -> 3.91 us  [shards(): pl.pallas_call(sum_body, grid=(steps,), out_shape=(jax.ShapeDtypeStruct((...]
where the time goes in v3:
time: 43.4 us; the launch traced here: 43.2 us
  Pallas kernels  42.6 us (98%)
  between operations  0.64 us (1%)
    pallas_call x1, Pallas kernels, shards(): pl.pallas_call(functools.partial(body, tiles, cols_of, rows, cols, cap),...  38.7 us
    pallas_call x1, Pallas kernels, shards(): pl.pallas_call(sum_body, grid=(steps,), out_shape=(jax.ShapeDtypeStruct((...  3.91 us

profile of v3, /device:TPU:9, one launch (start us, length us, event | category | flops | bytes accessed | tf_op | source)
XLA Modules:
  0.0 43.2 jit_solution(5058562853333877243)
XLA Ops:
  0.6 38.7 %quantize.1 = (bf16[512,256]{1,0:T(8,128)(2,1)}, f32[1,16]{1,0:T(1,128)}, f32[1,2048]{1,0:T(1,128)}, f32[8,8,128]{2,1,0:T(8,128)}, bf16[1024,256]{1,0:T(8,128)(2,1)}) custom-call(bf16[512,512]{1,0:T(8,128)(2,1)} %bitcast.12, bf16[4608,512]{1,0:T(8,128)(2,1)} %bitcast.10, f32[1,512]{1,0:T(1,128)} %bitcast.14, bf16[4608,256]{1,0:T(8,128)(2,1)} %bitcast.11, ...), custom_call_target="tpu_custom_call" | custom-call | tf_op jit(solution)/shard_map/quantize/pallas_call | solution.py:323
  39.3 3.9 %code_sums.1 = (bf16[512,256]{1,0:T(8,128)(2,1)}, f32[1,16]{1,0:T(1,128)}, f32[2048,256]{1,0:T(8,128)}, f32[1,2048]{1,0:T(1,128)}) custom-call(f32[8,8,128]{2,1,0:T(8,128)} %get-tuple-element.13.asked, bf16[1024,256]{1,0:T(8,128)(2,1)} %get-tuple-element.14.arrived, bf16[512,256]{1,0:T(8,128)(2,1)} %get-tuple-element.15.grad_in, ...), custom_call_target="tpu_custom_call" | custom-call | tf_op jit(solution)/shard_map/code_sums/pallas_call | solution.py:384
